TPU v7x, 512 devices: a whole 4x8x8 slice. The times are simulated.
512 devices in a mesh: dp: 8 (over y), ctx: 16 (over z_hi, x, core), head: 4 (over z_lo).
Axes of the slice: x: 4, y: 8, z: 8 (z_hi: 2, z_lo: 4; z = z_hi * 4 + z_lo), core: 2. Of those that a mesh axis runs over, the one named last changes fastest.
Arguments:
- queries: bfloat16 [65536, 3072], P(('dp', 'ctx'), 'head'), parts along dimension 0, may hold values from -6 to 6
- keys: bfloat16 [65536, 3072], P(('dp', 'ctx'), 'head'), parts along dimension 0, may hold values from -8 to 8
- values: bfloat16 [65536, 3072], P(('dp', 'ctx'), 'head'), parts along dimension 0, may hold values from -8 to 8
- pool_segments: int32 [128, 512], P(('dp', 'ctx')), parts along dimension 0, may hold values from 0 to 7, never falling along the last dimension, each value on 1 to 96 neighbouring positions
- window_map: int32 [128], P(('dp', 'ctx')), parts along dimension 0, may hold values from 0 to 15, each once
- ref_owner: int32 [8], P('dp'), parts along dimension 0, may hold values from 0 to 15
- ref_keys: bfloat16 [128, 512, 3072], P(('dp', 'ctx'), 'head'), parts along dimension 0, may hold values from -6 to 6
- ref_values: bfloat16 [128, 512, 3072], P(('dp', 'ctx'), 'head'), parts along dimension 0, may hold values from -6 to 6
- slopes: float32 [24], P('head'), may hold values from 0.02 to 2
Outputs:
- attended: bfloat16 [65536, 3072], P(('dp', 'ctx'), 'head'), parts along dimension 0
There are 8 independent parts, one for each index of `dp`. A program takes and returns all parts, laid end to end along the dimension named above; an argument that names none is the same for every part. Nothing has to cross between parts.
All inputs are finite; a program needn't handle non-finite values.
Results may differ from a plain program's by a relative error of at most 0.0021.
Values may be sent and summed in bfloat16 or wider, within the bound.
No kernel may reach another device: no remote copies, remote signals or barrier semaphores. Data moves between devices by JAX's collectives and lax.ppermute only.
A program may use at most 64 MiB of HBM per device.

v0:
```python
from functools import reduce
import math
import jax
import jax.numpy as jnp
from jax import lax
from jax.sharding import PartitionSpec as P

HD = 128
RATIO = 64


def spread(block, axis, source):
    block = jnp.where(lax.axis_index(axis) == source, block, jnp.zeros_like(block))
    return lax.psum(block, axis)


def group_terms(query_block, key_block, value_block, bias_term):
    score_scale = 1.0 / math.sqrt(HD)
    scores = (
        jnp.einsum("qhd,khd->hqk", query_block, key_block, preferred_element_type=jnp.float32)
        * score_scale
    )
    if bias_term is not None:
        scores = scores + bias_term[:, None, :]
    row_max = jnp.max(scores, axis=2)
    exp_terms = jnp.exp(scores - row_max[:, :, None])
    row_total = jnp.sum(exp_terms, axis=2)
    weights = exp_terms.astype(jnp.bfloat16)
    numerator = jnp.einsum("hqk,khd->qhd", weights, value_block, preferred_element_type=jnp.float32)
    return (row_max.T, row_total.T, numerator)


def combine_groups(group_list):
    ceiling = reduce(jnp.maximum, [triple[0] for triple in group_list])
    numerator = reduce(
        jnp.add, [jnp.exp(triple[0] - ceiling)[:, :, None] * triple[2] for triple in group_list]
    )
    denominator = reduce(
        jnp.add, [jnp.exp(triple[0] - ceiling) * triple[1] for triple in group_list]
    )
    return numerator / denominator[:, :, None]


def on_device(
    queries, keys, values, pool_segments, window_map, ref_owner, ref_keys, ref_values, slopes
):
    tok_rows = queries.shape[0]
    heads_here = queries.shape[1] // HD
    pool_count = tok_rows // RATIO
    member = (pool_segments[0][None, :] == jnp.arange(pool_count, dtype=jnp.int32)[:, None]).astype(
        jnp.bfloat16
    )
    counts = jnp.sum(member, axis=1, dtype=jnp.float32)
    pooled_keys = (
        jnp.dot(member, keys, preferred_element_type=jnp.float32) / counts[:, None]
    ).astype(jnp.bfloat16)
    pooled_values = (
        jnp.dot(member, values, preferred_element_type=jnp.float32) / counts[:, None]
    ).astype(jnp.bfloat16)
    window_tag = window_map.astype(jnp.bfloat16)
    all_keys, all_values, all_tags = (
        lax.all_gather(pooled_keys, "ctx", axis=0, tiled=True),
        lax.all_gather(pooled_values, "ctx", axis=0, tiled=True),
        lax.all_gather(window_tag, "ctx", axis=0, tiled=True),
    )
    ref_k, ref_v = (
        spread(ref_keys[0], "ctx", ref_owner[0]),
        spread(ref_values[0], "ctx", ref_owner[0]),
    )
    ref_k, ref_v = (
        lax.all_to_all(ref_k, "head", split_axis=1, concat_axis=0, tiled=True),
        lax.all_to_all(ref_v, "head", split_axis=1, concat_axis=0, tiled=True),
    )
    query_block = queries.reshape(tok_rows, heads_here, HD)
    key_block = keys.reshape(tok_rows, heads_here, HD)
    value_block = values.reshape(tok_rows, heads_here, HD)
    key_window = jnp.repeat(all_tags.astype(jnp.float32), pool_count)
    distance = jnp.abs(window_map[0].astype(jnp.float32) - key_window)
    bias_term = -slopes[:, None] * distance[None, :]
    group_list = [
        group_terms(query_block, key_block, value_block, None),
        group_terms(
            query_block,
            all_keys.reshape(-1, heads_here, HD),
            all_values.reshape(-1, heads_here, HD),
            bias_term,
        ),
        group_terms(
            query_block, ref_k.reshape(-1, heads_here, HD), ref_v.reshape(-1, heads_here, HD), None
        ),
    ]
    merged = combine_groups(group_list)
    return merged.reshape(tok_rows, heads_here * HD).astype(jnp.bfloat16)


def solution(mesh):
    return jax.shard_map(
        on_device,
        mesh=mesh,
        in_specs=(
            P(("dp", "ctx"), "head"),
            P(("dp", "ctx"), "head"),
            P(("dp", "ctx"), "head"),
            P(("dp", "ctx"), None),
            P(("dp", "ctx")),
            P("dp"),
            P(("dp", "ctx"), "head", None),
            P(("dp", "ctx"), "head", None),
            P("head"),
        ),
        out_specs=P(("dp", "ctx"), "head"),
        check_vma=False,
    )
```

profile of v0, /device:TPU:1, one launch (start us, length us, event | category | flops | bytes accessed | tf_op | source)
XLA Modules:
  0.0 324.7 jit_solution(16259391540248916373)
XLA Ops:
  6.5 0.0 all-reduce.4.cloned.1.call-start
  7.2 0.1 broadcast_select_fusion
  7.3 0.0 copy-start.7
  7.3 0.0 copy-start.1
  7.3 0.0 copy-start.6
  7.4 1.2 copy.74
  8.5 1.1 copy.65
  9.7 0.0 all-reduce.4.cloned.1.call-update
  10.4 1.3 dynamic-slice
  11.8 0.7 dynamic-update-slice
  12.5 49.1 %all-reduce = bf16[16]{0:T(256)(128)(2,1)S(1)} all-reduce(bf16[16]{0:T(256)(128)(2,1)S(1)} %dynamic-update-slice), channel_id=1, replica_groups=mesh['dp'=8,'ctx'=16,'head'=4] {'ctx'}, use_global_device_ids=true, to_apply=%add | all-reduce | flops 16 | bytes 64
  61.6 0.0 copy-done.7
  61.6 0.1 broadcast_in_dim.2
  61.7 0.1 abs.12
  61.8 0.0 copy-done.1
  61.8 1.3 copy.59
  63.0 0.0 copy-done.6
  63.0 0.1 convert_reduce_fusion
  63.1 141.0 %all-reduce.4.cloned.1.call-done = (bf16[128,4,768]{0,2,1:T(8,128)(2,1)}, bf16[128,4,768]{0,2,1:T(8,128)(2,1)}) async-done(((bf16[128,4,768]{0,2,1:T(8,128)(2,1)}, bf16[128,4,768]{0,2,1:T(8,128)(2,1)}), (bf16[128,4,768]{0,2,1:T(8,128)(2,1)}, bf16[128,4,768]{0,2,1:T(8,128)(2,1)})) %all-reduce.4.cloned.1.call-update) | async-done | bytes 1572880 | tf_op jit(solution)/shard_map/psum | solution.py:14
  204.2 4.2 %all-to-all-start.1 = ((bf16[128,4,768]{0,2,1:T(8,128)(2,1)}), bf16[128,4,768]{0,2,1:T(8,128)(2,1)}, u32[]{:S(2)}, u32[]{:S(2)}) async-start(bf16[128,4,768]{0,2,1:T(8,128)(2,1)} %get-tuple-element.5), calls=%async_computation.1 | async-start | bytes 1572864 | tf_op jit(solution)/shard_map/all_to_all | solution.py:72
  208.4 0.2 fusion.20
  208.6 36.4 %all_gather.9 = bf16[128,768]{1,0:T(8,128)(2,1)S(1)} all-gather(bf16[8,768]{1,0:T(8,128)(2,1)S(1)} %fusion.20), channel_id=1, replica_groups=mesh['dp'=8,'ctx'=16,'head'=4] {'ctx'}, dimensions={0}, use_global_device_ids=true | all-gather | bytes 208896 | tf_op jit(solution)/shard_map/all_gather | solution.py:62
  245.0 0.2 copy.62
  245.1 0.3 copy.58
  245.4 0.1 broadcast_multiply_fusion
  245.5 1.0 bitcast_reduce_fusion.1
  246.5 4.9 %multiply_reduce_fusion = (f32[6,512]{1,0:T(8,128)S(1)}, f32[6,512,512]{1,2,0:T(8,128)}) fusion(bf16[512,6,128]{0,2,1:T(8,128)(2,1)S(1)} %bitcast.127, bf16[512,6,128]{0,2,1:T(8,128)(2,1)} %bitcast.132), kind=kOutput, calls=%fused_computation.4 | convolution fusion | flops 405795840 | bytes 7876608 | tf_op jit(solution)/shard_map/qhd,khd->hqk/dot_general | solution.py:20
  251.4 0.0 all-to-all-done.1
  251.4 4.5 %all-to-all-start = ((bf16[128,4,768]{0,2,1:T(8,128)(2,1)}), bf16[128,4,768]{0,2,1:T(8,128)(2,1)}, u32[]{:S(2)}, u32[]{:S(2)}) async-start(bf16[128,4,768]{0,2,1:T(8,128)(2,1)} %get-tuple-element.6), calls=%async_computation | async-start | bytes 1572864 | tf_op jit(solution)/shard_map/all_to_all | solution.py:71
  255.9 0.2 fusion.21
  256.1 1.4 copy.70
  257.5 35.2 %all_gather.11 = bf16[128,768]{1,0:T(8,128)(2,1)S(1)} all-gather(bf16[8,768]{1,0:T(8,128)(2,1)S(1)} %fusion.21), channel_id=1, replica_groups=mesh['dp'=8,'ctx'=16,'head'=4] {'ctx'}, dimensions={0}, use_global_device_ids=true | all-gather | bytes 208896 | tf_op jit(solution)/shard_map/all_gather | solution.py:63
  292.8 0.2 copy.72
  292.9 1.0 fusion.18
  293.9 4.0 %fusion.1 = f32[6,512]{1,0:T(8,128)S(1)} fusion(f32[6,512,512]{1,2,0:T(8,128)} %get-tuple-element.14, f32[6,512]{1,0:T(8,128)S(1)} %get-tuple-element.13), kind=kLoop, calls=%fused_computation.5 | loop fusion | flops 4715520 | bytes 6316032 | tf_op jit(solution)/shard_map/reduce_sum | solution.py:27
  297.9 0.6 copy-done
  298.5 2.5 fusion.7
  300.9 2.6 copy.75
  303.6 1.6 reshape.86
  305.2 0.0 all-to-all-done
  305.2 2.6 copy.66
  307.9 2.4 reshape.83
  310.2 2.2 bitcast_reduce_fusion
  312.5 1.6 fusion.3
  314.1 1.9 fusion.5
  316.1 0.0 copy-done.3
  316.1 0.6 fusion.15
  316.7 1.2 copy.76
  (12 shorter events, 0.1 us)
Async XLA Ops:
  6.5 197.6 %all-reduce.4.cloned.1.call-start = ((), (), s32[]{:S(2)}) async-start(), calls=%async_computation.2 | async-start | bytes 3145728 | tf_op jit(solution)/shard_map/psum | solution.py:14
  7.3 54.3 %copy-start.7 = (f32[6]{0:T(128)S(1)}, f32[6]{0:T(128)}, u32[]{:S(2)}) copy-start(f32[6]{0:T(128)} %param.17) | copy-start | bytes 76
  7.3 54.4 %copy-start.1 = (bf16[512,768]{1,0:T(8,128)(2,1)S(1)}, bf16[512,768]{1,0:T(8,128)(2,1)}, u32[]{:S(2)}) copy-start(bf16[512,768]{1,0:T(8,128)(2,1)} %param.10) | copy-start | bytes 2359300
  7.3 55.7 %copy-start.6 = (s32[1,512]{1,0:T(1,128)S(1)}, s32[1,512]{1,0:T(1,128)}, u32[]{:S(2)}) copy-start(s32[1,512]{1,0:T(1,128)} %param.12) | copy-start | bytes 6148
  9.7 235.5 %copy-start.4 = (bf16[512,768]{1,0:T(8,128)(2,1)S(1)}, bf16[512,768]{1,0:T(8,128)(2,1)}, u32[]{:S(2)}) copy-start(bf16[512,768]{1,0:T(8,128)(2,1)} %param.9) | copy-start | bytes 2359300
  204.2 47.2 %all-to-all-start.1 = ((bf16[128,4,768]{0,2,1:T(8,128)(2,1)}), bf16[128,4,768]{0,2,1:T(8,128)(2,1)}, u32[]{:S(2)}, u32[]{:S(2)}) async-start(bf16[128,4,768]{0,2,1:T(8,128)(2,1)} %get-tuple-element.5), calls=%async_computation.1 | async-start | bytes 1572864 | tf_op jit(solution)/shard_map/all_to_all | solution.py:72
  246.5 9.4 %copy-start.2 = (bf16[512,768]{1,0:T(8,128)(2,1)S(1)}, bf16[512,768]{1,0:T(8,128)(2,1)}, u32[]{:S(2)}) copy-start(bf16[512,768]{1,0:T(8,128)(2,1)} %param.11) | copy-start | bytes 2359300
  251.4 53.8 %all-to-all-start = ((bf16[128,4,768]{0,2,1:T(8,128)(2,1)}), bf16[128,4,768]{0,2,1:T(8,128)(2,1)}, u32[]{:S(2)}, u32[]{:S(2)}) async-start(bf16[128,4,768]{0,2,1:T(8,128)(2,1)} %get-tuple-element.6), calls=%async_computation | async-start | bytes 1572864 | tf_op jit(solution)/shard_map/all_to_all | solution.py:71
  293.9 4.6 %copy-start = (f32[6,512,512]{1,2,0:T(8,128)S(1)}, f32[6,512,512]{1,2,0:T(8,128)}, u32[]{:S(2)}) copy-start(f32[6,512,512]{1,2,0:T(8,128)} %get-tuple-element.14) | copy-start | bytes 18874372
  314.1 2.0 copy-start.5
  314.1 2.0 copy-start.3
Sparse Core Ops, SparseCore 0:
  10.3 193.8 all-reduce.3
where the time goes:
time: 325 us
  waiting for transfers between devices  141 us (43%)
  blocking collectives  121 us (37%)
  local copies, waits for them, and re-layouts  18.9 us (6%)
  between operations  15 us (5%)
  matrix products  13.6 us (4%)
  starting transfers between devices  8.65 us (3%)
  other arithmetic  6.88 us (2%)
    psum x1, waiting for transfers between devices, spread(): return lax.psum(block, axis)  141 us
    unnamed x1, blocking collectives  49.1 us
    all_gather x1, blocking collectives, on_device(): lax.all_gather(pooled_keys, 'ctx', axis=0, tiled=True)  36.4 us
    all_gather x1, blocking collectives, on_device(): lax.all_gather(pooled_values, 'ctx', axis=0, tiled=True)  35.2 us
    dot_general x3, matrix products, group_terms(): jnp.einsum('qhd,khd->hqk', query_block, key_block, preferred_element_type...  8.16 us
    reduce_sum x3, other arithmetic, group_terms(): row_total = jnp.sum(exp_terms, axis=2)  6.54 us
  transfers between devices with their start and end apart: 3, of which 1 were waited for; matrix products, arithmetic and copies ran while one was open for 7% of the time, Pallas kernels for 0%

commit v1 on v0

--- a/solution.py
+++ b/solution.py
@@ -58,9 +58,12 @@
         jnp.dot(member, values, preferred_element_type=jnp.float32) / counts[:, None]
     ).astype(jnp.bfloat16)
     window_tag = window_map.astype(jnp.bfloat16)
+    recast_sample_by_axis = lambda payload: jnp.concatenate(
+        lax.all_to_all(jnp.stack([payload] * lax.axis_size("ctx"), axis=0), "ctx", 0, 0), axis=0
+    )
     all_keys, all_values, all_tags = (
         lax.all_gather(pooled_keys, "ctx", axis=0, tiled=True),
-        lax.all_gather(pooled_values, "ctx", axis=0, tiled=True),
+        recast_sample_by_axis(pooled_values),
         lax.all_gather(window_tag, "ctx", axis=0, tiled=True),
     )
     ref_k, ref_v = (

time: 325 us -> 293 us (0.902)
  blocking collectives: 121 us -> 79.3 us
  starting transfers between devices: 8.65 us -> 23.9 us
    all_gather x1 -> x0, blocking collectives: 35.2 us -> none  [on_device(): lax.all_gather(pooled_values, 'ctx', axis=0, tiled=True)]
    all_to_all x0 -> x1, starting transfers between devices: none -> 15.1 us  [on_device(): lax.all_to_all(jnp.stack([payload] * lax.axis_size('ctx'), axis=0), 'ctx'...]
    psum x1, waiting for transfers between devices: 141 us -> 132 us  [spread(): return lax.psum(block, axis)]
    unnamed x1, blocking collectives: 49.1 us -> 43.4 us
    all_to_all x1, waiting for transfers between devices: 0.01 us -> 5.54 us  [on_device(): lax.all_to_all(ref_k, 'head', split_axis=1, concat_axis=0, tiled=True)]
  transfers between devices with their start and end apart: 3 -> 4, of which waited for: 1 -> 2; matrix products, arithmetic and copies ran while one was open for 7% -> 8% of each run, Pallas kernels for 0% -> 0%
where the time goes in v1:
time: 293 us; the launch traced here: 292 us
  waiting for transfers between devices  138 us (47%)
  blocking collectives  79.3 us (27%)
  starting transfers between devices  23.9 us (8%)
  local copies, waits for them, and re-layouts  15.8 us (5%)
  between operations  14.9 us (5%)
  matrix products  12.9 us (4%)
  other arithmetic  7.64 us (3%)
    psum x1, waiting for transfers between devices, spread(): return lax.psum(block, axis)  132 us
    unnamed x1, blocking collectives  43.4 us
    all_gather x1, blocking collectives, on_device(): lax.all_gather(pooled_keys, 'ctx', axis=0, tiled=True)  35.9 us
    all_to_all x1, starting transfers between devices, on_device(): lax.all_to_all(jnp.stack([payload] * lax.axis_size('ctx'), axis=0), 'ctx'...  15.1 us
    dot_general x3, matrix products, group_terms(): jnp.einsum('qhd,khd->hqk', query_block, key_block, preferred_element_type...  7.47 us
    reduce_sum x3, other arithmetic, group_terms(): row_total = jnp.sum(exp_terms, axis=2)  7.29 us
    unnamed x24, local copies, waits for them, and re-layouts  6.07 us
  transfers between devices with their start and end apart: 4, of which 2 were waited for; matrix products, arithmetic and copies ran while one was open for 8% of the time, Pallas kernels for 0%

profile of v1, /device:TPU:1, one launch (start us, length us, event | category | flops | bytes accessed | tf_op | source)
XLA Modules:
  0.0 292.3 jit_solution(15864039277835257652)
XLA Ops:
  6.5 0.0 all-reduce.4.cloned.1.call-start
  7.2 0.1 broadcast_select_fusion
  7.3 0.0 copy-start.5
  7.3 0.0 copy-start.3
  7.3 0.0 copy-start.6
  7.4 1.2 copy.74
  8.5 1.2 copy.65
  9.7 0.0 all-reduce.4.cloned.1.call-update
  9.7 0.0 copy-done.5
  9.7 0.1 convert_reduce_fusion
  9.8 0.0 copy-done.3
  9.8 0.2 fusion.21
  10.0 0.7 stack.2
  10.7 15.1 %all-to-all-start.1 = ((bf16[16,8,768]{2,1,0:T(8,128)(2,1)}), bf16[16,8,768]{2,1,0:T(8,128)(2,1)S(1)}, u32[]{:S(2)}, u32[]{:S(2)}) async-start(bf16[16,8,768]{2,1,0:T(8,128)(2,1)} %stack.2), calls=%async_computation.1 | async-start | bytes 393216 | tf_op jit(solution)/shard_map/all_to_all | solution.py:62
  26.4 1.3 dynamic-slice
  27.7 0.7 dynamic-update-slice
  28.5 43.4 %all-reduce = bf16[16]{0:T(256)(128)(2,1)S(1)} all-reduce(bf16[16]{0:T(256)(128)(2,1)S(1)} %dynamic-update-slice), channel_id=1, replica_groups=mesh['dp'=8,'ctx'=16,'head'=4] {'ctx'}, use_global_device_ids=true, to_apply=%add | all-reduce | flops 16 | bytes 64
  71.9 0.0 all-to-all-done.1
  71.9 132.4 %all-reduce.4.cloned.1.call-done = (bf16[128,4,768]{0,2,1:T(8,128)(2,1)}, bf16[128,4,768]{0,2,1:T(8,128)(2,1)}) async-done(((bf16[128,4,768]{0,2,1:T(8,128)(2,1)}, bf16[128,4,768]{0,2,1:T(8,128)(2,1)}), (bf16[128,4,768]{0,2,1:T(8,128)(2,1)}, bf16[128,4,768]{0,2,1:T(8,128)(2,1)})) %all-reduce.4.cloned.1.call-update) | async-done | bytes 1572880 | tf_op jit(solution)/shard_map/psum | solution.py:14
  204.3 4.2 %all-to-all-start.2 = ((bf16[128,4,768]{0,2,1:T(8,128)(2,1)}), bf16[128,4,768]{0,2,1:T(8,128)(2,1)}, u32[]{:S(2)}, u32[]{:S(2)}) async-start(bf16[128,4,768]{0,2,1:T(8,128)(2,1)} %get-tuple-element.5), calls=%async_computation.2 | async-start | bytes 1572864 | tf_op jit(solution)/shard_map/all_to_all | solution.py:75
  208.5 0.1 broadcast_in_dim.2
  208.6 0.1 abs.12
  208.7 0.3 copy.59
  208.9 0.2 fusion.20
  209.1 35.9 %all_gather.6 = bf16[128,768]{1,0:T(8,128)(2,1)S(1)} all-gather(bf16[8,768]{1,0:T(8,128)(2,1)S(1)} %fusion.20), channel_id=1, replica_groups=mesh['dp'=8,'ctx'=16,'head'=4] {'ctx'}, dimensions={0}, use_global_device_ids=true | all-gather | bytes 208896 | tf_op jit(solution)/shard_map/all_gather | solution.py:65
  245.0 0.2 copy.62
  245.2 1.4 copy.58
  246.6 0.1 broadcast_multiply_fusion
  246.7 3.7 %multiply_reduce_fusion = (f32[6,512]{1,0:T(8,128)S(1)}, f32[6,512,512]{1,2,0:T(8,128)}) fusion(bf16[512,6,128]{0,2,1:T(8,128)(2,1)S(1)} %bitcast.126, bf16[512,6,128]{0,2,1:T(8,128)(2,1)S(1)} %bitcast.132), kind=kOutput, calls=%fused_computation.4 | convolution fusion | flops 405795840 | bytes 7876608 | tf_op jit(solution)/shard_map/qhd,khd->hqk/dot_general | solution.py:20
  250.4 0.0 all-to-all-done.2
  250.4 4.6 %all-to-all-start = ((bf16[128,4,768]{0,2,1:T(8,128)(2,1)}), bf16[128,4,768]{0,2,1:T(8,128)(2,1)}, u32[]{:S(2)}, u32[]{:S(2)}) async-start(bf16[128,4,768]{0,2,1:T(8,128)(2,1)} %get-tuple-element.6), calls=%async_computation | async-start | bytes 1572864 | tf_op jit(solution)/shard_map/all_to_all | solution.py:74
  255.0 1.6 bitcast_reduce_fusion.1
  256.6 2.3 copy.70
  258.9 1.8 fusion.18
  260.7 0.0 copy-start.1
  260.7 3.9 %fusion.1 = f32[6,512]{1,0:T(8,128)S(1)} fusion(f32[6,512,512]{1,2,0:T(8,128)} %get-tuple-element.14, f32[6,512]{1,0:T(8,128)S(1)} %get-tuple-element.13), kind=kLoop, calls=%fused_computation.5 | loop fusion | flops 4715520 | bytes 6316032 | tf_op jit(solution)/shard_map/reduce_sum | solution.py:27
  264.6 2.5 fusion.7
  267.1 0.2 reshape_reshape.3
  267.3 1.7 copy.75
  269.1 0.3 reshape.84
  269.4 5.5 %all-to-all-done = bf16[128,4,768]{0,2,1:T(8,128)(2,1)} async-done(((bf16[128,4,768]{0,2,1:T(8,128)(2,1)}), bf16[128,4,768]{0,2,1:T(8,128)(2,1)}, u32[]{:S(2)}, u32[]{:S(2)}) %all-to-all-start) | async-done | bytes 786464 | tf_op jit(solution)/shard_map/all_to_all | solution.py:74
  274.9 1.7 copy.66
  276.6 1.2 reshape.82
  277.8 2.2 bitcast_reduce_fusion
  280.1 1.6 fusion.3
  281.7 1.9 fusion.5
  283.7 0.6 fusion.15
  284.3 1.2 copy.76
  (17 shorter events, 0.1 us)
Async XLA Ops:
  6.5 197.7 %all-reduce.4.cloned.1.call-start = ((), (), s32[]{:S(2)}) async-start(), calls=%async_computation.3 | async-start | bytes 3145728 | tf_op jit(solution)/shard_map/psum | solution.py:14
  7.3 2.4 copy-start.5
  7.3 2.5 copy-start.3
  7.3 64.5 %copy-start.6 = (f32[6]{0:T(128)S(1)}, f32[6]{0:T(128)}, u32[]{:S(2)}) copy-start(f32[6]{0:T(128)} %param.17) | copy-start | bytes 76
  8.5 200.1 %copy-start.2 = (bf16[512,768]{1,0:T(8,128)(2,1)S(1)}, bf16[512,768]{1,0:T(8,128)(2,1)}, u32[]{:S(2)}) copy-start(bf16[512,768]{1,0:T(8,128)(2,1)} %param.10) | copy-start | bytes 2359300
  10.7 61.1 %all-to-all-start.1 = ((bf16[16,8,768]{2,1,0:T(8,128)(2,1)}), bf16[16,8,768]{2,1,0:T(8,128)(2,1)S(1)}, u32[]{:S(2)}, u32[]{:S(2)}) async-start(bf16[16,8,768]{2,1,0:T(8,128)(2,1)} %stack.2), calls=%async_computation.1 | async-start | bytes 393216 | tf_op jit(solution)/shard_map/all_to_all | solution.py:62
  204.3 46.1 %all-to-all-start.2 = ((bf16[128,4,768]{0,2,1:T(8,128)(2,1)}), bf16[128,4,768]{0,2,1:T(8,128)(2,1)}, u32[]{:S(2)}, u32[]{:S(2)}) async-start(bf16[128,4,768]{0,2,1:T(8,128)(2,1)} %get-tuple-element.5), calls=%async_computation.2 | async-start | bytes 1572864 | tf_op jit(solution)/shard_map/all_to_all | solution.py:75
  250.4 14.2 %slice-start = ((s8[6291456]{0:T(1024)(128)(4,1)}), s8[2097152]{0:T(1024)(128)(4,1)S(1)}, s32[]{:S(2)}) async-start(s8[6291456]{0:T(1024)(128)(4,1)} %bitcast.124), calls=%async_computation.4 | async-start | bytes 4194304
  250.4 24.5 %all-to-all-start = ((bf16[128,4,768]{0,2,1:T(8,128)(2,1)}), bf16[128,4,768]{0,2,1:T(8,128)(2,1)}, u32[]{:S(2)}, u32[]{:S(2)}) async-start(bf16[128,4,768]{0,2,1:T(8,128)(2,1)} %get-tuple-element.6), calls=%async_computation | async-start | bytes 1572864 | tf_op jit(solution)/shard_map/all_to_all | solution.py:74
  258.9 5.7 %slice-start.1 = ((s8[6291456]{0:T(1024)(128)(4,1)}), s8[4194304]{0:T(1024)(128)(4,1)S(1)}, s32[]{:S(2)}) async-start(s8[6291456]{0:T(1024)(128)(4,1)} %bitcast.124), calls=%async_computation.5 | async-start | bytes 8388608
  260.7 3.9 %copy-start.1 = (bf16[512,768]{0,1:T(8,128)(2,1)S(1)}, bf16[512,768]{0,1:T(8,128)(2,1)}, u32[]{:S(2)}) copy-start(bf16[512,768]{0,1:T(8,128)(2,1)} %copy.70) | copy-start | bytes 2359300
  281.7 2.0 copy-start
  281.7 2.0 copy-start.4
Sparse Core Ops, SparseCore 0:
  10.3 193.8 all-reduce.3
